TPU v7x, 512 devices: a whole 4x8x8 slice. The times are simulated.
512 devices in a mesh: dp: 16 (over z, core), fsdp: 4 (over x), tensor: 8 (over y).
Axes of the slice: x: 4, y: 8, z: 8, core: 2. Of those that a mesh axis runs over, the one named last changes fastest.
Arguments:
- tokens: bfloat16 [16384, 8192], P(('dp', 'fsdp'), 'tensor'), may hold values from -700 to 700
- queries: bfloat16 [16384, 8192], P(('dp', 'fsdp'), 'tensor'), may hold values from -140 to 140
- segment_ids: int32 [128, 128], P(('dp', 'fsdp')), may hold values from 0 to 3, never falling along the last dimension, each value on 1 to 64 neighbouring positions
- gain: float32 [8192], P('tensor'), may hold values from 0.1 to 1.9
- key_value_weight: bfloat16 [8192, 2048], P('tensor', 'fsdp'), may hold values from -0.0625 to 0.0625
- plan: int32 [32], replicated, may hold values from 0 to 31, as said below
Outputs:
- attended: bfloat16 [16384, 8192], P(('dp', 'fsdp'), 'tensor')
Inputs may be any that keep to these rules, and one draw needn't show every extreme that they name: plan is a permutation of 0 to 31; from one dp index to another at most 1 micro-batches go, and in every draw some pair of dp indices carries exactly 1.
All inputs are finite; a program needn't handle non-finite values.
Results may differ from a plain program's by a relative error of at most 0.011.
Values may be sent and summed in bfloat16 or wider, within the bound.
No kernel may reach another device: no remote copies, remote signals or barrier semaphores. Data moves between devices by JAX's collectives and lax.ppermute only.
A program may use at most 64 MiB of HBM per device.

v0:
```python
import jax
import jax.numpy as jnp
from jax import lax
from jax.sharding import PartitionSpec as P

HEAD_SIZE = 128
epsilon = 1e-05


def total_of_pieces(array, axis):
    parts = lax.all_gather(array, axis)
    return parts.sum(axis=0)


def pack_rows(send_index, send_valid, flat_rows, length):
    ranks_here = send_index.shape[0]
    slots_here = send_index.shape[1]
    taken = jnp.take(flat_rows, send_index.reshape(-1), axis=0)
    sent = taken * send_valid.astype(flat_rows.dtype)
    return sent.reshape(ranks_here, slots_here, length, -1)


def unpack_rows(keep_index, arrived):
    flat = arrived.reshape(arrived.shape[0] * arrived.shape[1], -1)
    return jnp.take(flat, keep_index, axis=0)


def project(rows, gain, key_value_weight):
    values = rows.astype(jnp.float32)
    stats = total_of_pieces(jnp.sum(values * values, axis=1), "tensor")
    full_width = rows.shape[1] * lax.axis_size("tensor")
    scale = lax.rsqrt(stats / full_width + epsilon)
    normed = (values * scale[:, None] * gain).astype(jnp.bfloat16)
    partial_value = jnp.dot(
        normed,
        lax.all_gather(key_value_weight, "fsdp", axis=1, tiled=True),
        preferred_element_type=jnp.float32,
    )
    return lax.psum_scatter(partial_value, "tensor", scatter_dimension=1, tiled=True)


def attend(query_row_block, key_value_rows, documents):
    batches, length = documents.shape
    heads_kv = key_value_rows.shape[1] // (2 * HEAD_SIZE)
    head_group = query_row_block.shape[1] // (heads_kv * HEAD_SIZE)
    query_head_count = query_row_block.astype(jnp.float32).reshape(
        batches, length, heads_kv, head_group, HEAD_SIZE
    )
    key_value_heads = key_value_rows.reshape(batches, length, heads_kv, 2, HEAD_SIZE)
    scores = jnp.einsum(
        "mqhgd,mkhd->mhgqk",
        query_head_count,
        key_value_heads[:, :, :, 0],
        precision=lax.Precision.HIGHEST,
    ) * HEAD_SIZE ** (-0.5)
    positions = jnp.arange(length, dtype=jnp.int32)
    causal = positions[:, None] >= positions[None, :]
    allowed = (documents[:, :, None] == documents[:, None, :]) & causal[None]
    scores = jnp.where(allowed[:, None, None], scores, -1e30)
    row_max = jnp.max(scores, axis=-1, keepdims=True)
    expo = jnp.exp(scores - row_max)
    weights = (expo / jnp.sum(expo, axis=-1, keepdims=True)).astype(jnp.bfloat16)
    mixed = jnp.einsum(
        "mhgqk,mkhd->mqhgd",
        weights.astype(jnp.float32),
        key_value_heads[:, :, :, 1],
        precision=lax.Precision.HIGHEST,
    )
    return mixed.reshape(batches * length, -1).astype(jnp.bfloat16)


def shards(tokens, queries, segment_ids, gain, key_value_weight, plan):
    rank_count = lax.axis_size("dp")
    own_rank = lax.axis_index("dp")
    batches = segment_ids.shape[0]
    length = segment_ids.shape[1]
    slot_cap = (batches + rank_count - 1) // rank_count
    dest_rank = plan.reshape(rank_count, batches) // batches
    slot_range = jnp.arange(batches, dtype=jnp.int32)
    same_dest = dest_rank[:, :, None] == dest_rank[:, None, :]
    earlier = slot_range[None, None, :] < slot_range[None, :, None]
    arrival = jnp.sum((same_dest & earlier).astype(jnp.int32), axis=2)
    own_dest = lax.dynamic_index_in_dim(dest_rank, own_rank, 0, keepdims=False)
    own_arrival = lax.dynamic_index_in_dim(arrival, own_rank, 0, keepdims=False)
    rank_range = jnp.arange(rank_count, dtype=jnp.int32)
    cap_range = jnp.arange(slot_cap, dtype=jnp.int32)
    send_hits = (
        (own_dest[None, None, :] == rank_range[:, None, None])
        & (own_arrival[None, None, :] == cap_range[None, :, None])
    ).astype(jnp.int32)
    send_index = jnp.sum(send_hits * slot_range[None, None, :], axis=2)
    send_valid = jnp.sum(send_hits, axis=2)
    inverse = jnp.argsort(plan)
    sources = lax.dynamic_slice_in_dim(inverse, own_rank * batches, batches)
    source_rank = sources // batches
    source_arrival = jnp.take(arrival.reshape(-1), sources)
    keep_index = source_rank * slot_cap + source_arrival
    local_kv = project(tokens, gain, key_value_weight)
    results = attend(queries, local_kv, segment_ids)
    parcel = pack_rows(send_index, send_valid, results.reshape(batches, -1), length)
    arrived = lax.all_to_all(parcel, "dp", split_axis=0, concat_axis=0, tiled=True)
    return unpack_rows(keep_index, arrived).reshape(batches * length, -1)


def solution(mesh):
    placed = (
        P(("dp", "fsdp"), "tensor"),
        P(("dp", "fsdp"), "tensor"),
        P(("dp", "fsdp"), None),
        P("tensor"),
        P("tensor", "fsdp"),
        P(),
    )
    return jax.shard_map(
        shards, mesh=mesh, in_specs=placed, out_specs=P(("dp", "fsdp"), "tensor"), check_vma=False
    )
```

profile of v0, /device:TPU:1, one launch (start us, length us, event | category | flops | bytes accessed | tf_op | source)
XLA Modules:
  0.0 254.4 jit_solution(3766419235261938822)
XLA Ops:
  6.5 0.7 all-gather.4.cloned.1.call-update
  7.3 1.2 fusion.4
  8.5 13.8 %all-gather.1 = f32[8,1,256]{2,1,0:T(1,128)S(1)} all-gather(f32[1,1,256]{2,1,0:T(1,128)S(1)} %bitcast.63), channel_id=2, replica_groups=mesh['dp'=16,'fsdp'=4,'tensor'=8] {'tensor'}, dimensions={0}, use_global_device_ids=true | all-gather | bytes 9216 | tf_op jit(solution)/shard_map/all_gather | solution.py:11
  22.4 46.1 %all-gather.4.cloned.1.call-done = bf16[1024,2048]{1,0:T(8,128)(2,1)} async-done(((bf16[1024,512]{1,0:T(8,128)(2,1)}), bf16[1024,2048]{1,0:T(8,128)(2,1)}) %all-gather.4.cloned.1.call-update) | async-done | bytes 4194320 | tf_op jit(solution)/shard_map/all_gather | solution.py:36
  68.5 5.0 %fusion.8 = f32[256,2048]{1,0:T(8,128)} fusion(bf16[1024,2048]{1,0:T(8,128)(2,1)} %all-gather.4.cloned.1.call-done, bf16[256,1024]{1,0:T(8,128)(2,1)} %param.6, f32[1024]{0:T(1024)} %param.9, f32[256]{0:T(256)S(1)} %add_rsqrt_fusion), kind=kOutput, calls=%fused_computation.21 | convolution fusion | flops 1074790400 | bytes 6820864 | tf_op jit(solution)/shard_map/dot_general | solution.py:34
  74.0 0.2 compare_reduce_fusion
  74.4 0.1 compare_and_fusion
  74.5 40.1 %reduce-scatter.2.cloned.1.call-done = f32[256,256]{1,0:T(8,128)} async-done(((f32[256,2048]{1,0:T(8,128)}), f32[256,256]{1,0:T(8,128)}) %reduce-scatter.2.cloned.1.call-update) | async-done | bytes 262160 | tf_op jit(solution)/shard_map/reduce_scatter | solution.py:39
  114.5 1.1 reshape.341
  115.6 0.2 fusion.21
  115.8 0.7 fusion.22
  116.5 0.2 fusion.7
  116.7 0.6 fusion.3
  117.3 0.3 copy.29
  117.6 0.1 convert_element_type.53
  117.8 0.4 fusion.20
  118.2 1.9 gather_fusion.1
  120.1 3.3 %gather_fusion.2 = bf16[16,65536]{1,0:T(8,128)(2,1)} fusion(bf16[2,65536]{1,0:T(2,128)(2,1)S(1)} %get-tuple-element.14, s32[1024]{0:T(1024)S(1)} %pad_clamp_fusion.1), kind=kCustom, calls=%fused_computation.2 | custom fusion | bytes 4194368 | tf_op jit(solution)/shard_map/jit(_take)/gather | solution.py:18
  123.4 1.9 pad_maximum_fusion
  125.3 2.3 copy.37
  127.6 2.6 %fusion = bf16[16,1,128,1024]{3,2,1,0:T(8,128)(2,1)} fusion(pred[16]{0:T(512)(128)(4,1)S(1)} %compare_and_fusion.1, bf16[16]{0:T(256)(128)(2,1)S(1)} %convert_element_type.55, bf16[2,8,128,1024]{3,2,1,0:T(8,128)(2,1)S(1)} %copy.37), kind=kLoop, calls=%fused_computation.7 | loop fusion | flops 4194304 | bytes 8388656 | tf_op jit(solution)/shard_map/mul | solution.py:19
  130.2 11.9 %all-to-all-start = ((bf16[16,1,128,1024]{3,2,1,0:T(8,128)(2,1)}), bf16[16,1,128,1024]{3,2,1,0:T(8,128)(2,1)}, u32[]{:S(2)}, u32[]{:S(2)}) async-start(bf16[16,1,128,1024]{3,2,1,0:T(8,128)(2,1)} %fusion), calls=%async_computation.1 | async-start | bytes 8388608 | tf_op jit(solution)/shard_map/all_to_all | solution.py:101
  142.2 1.6 sort.17
  144.0 0.6 gather_fusion
  144.8 90.9 %all-to-all-done = bf16[16,1,128,1024]{3,2,1,0:T(8,128)(2,1)} async-done(((bf16[16,1,128,1024]{3,2,1,0:T(8,128)(2,1)}), bf16[16,1,128,1024]{3,2,1,0:T(8,128)(2,1)}, u32[]{:S(2)}, u32[]{:S(2)}) %all-to-all-start) | async-done | bytes 4194336 | tf_op jit(solution)/shard_map/all_to_all | solution.py:101
  235.7 4.5 %copy.38 = bf16[2,8,128,1024]{3,1,2,0:T(8,128)(2,1)S(1)} copy(bf16[2,8,128,1024]{3,2,1,0:T(8,128)(2,1)} %bitcast.36) | data formatting | bytes 8388608
  240.2 1.6 fusion.19
  241.8 3.0 %gather_fusion.3 = bf16[2,65536]{1,0:T(2,128)(2,1)S(1)} fusion(bf16[16,65536]{1,0:T(8,128)(2,1)} %get-tuple-element.11, s32[1024]{0:T(1024)S(1)} %pad_clamp_fusion), kind=kCustom, calls=%fused_computation.3 | custom fusion | bytes 524296 | tf_op jit(solution)/shard_map/jit(_take)/gather | solution.py:25
  244.8 0.9 gather_fusion.4
  245.7 0.5 pad_maximum_fusion.1
  246.2 0.5 gather.20
  246.7 0.9 broadcast_select_fusion
  (32 shorter events, 1.0 us)
Async XLA Ops:
  6.5 62.0 %all-gather.4.cloned.1.call-start = ((), (), s32[]{:S(2)}) async-start(), calls=%async_computation.2 | async-start | bytes 5242880 | tf_op jit(solution)/shard_map/all_gather | solution.py:36
  7.3 107.3 %reduce-scatter.2.cloned.1.call-start = ((), (), s32[]{:S(2)}) async-start(), calls=%async_computation.3 | async-start | bytes 2359296 | tf_op jit(solution)/shard_map/reduce_scatter | solution.py:39
  22.4 51.2 %copy-start.2 = (s32[32]{0:T(128)S(1)}, s32[32]{0:T(128)}, u32[]{:S(2)}) copy-start(s32[32]{0:T(128)} %param.11) | copy-start | bytes 388
  22.4 51.4 %copy-start = (bf16[256,1024]{1,0:T(8,128)(2,1)S(1)}, bf16[256,1024]{1,0:T(8,128)(2,1)}, u32[]{:S(2)}) copy-start(bf16[256,1024]{1,0:T(8,128)(2,1)} %param.7) | copy-start | bytes 1572868
  22.4 51.9 %copy-start.1 = (s32[2,128]{1,0:T(2,128)S(1)}, s32[2,128]{1,0:T(2,128)}, u32[]{:S(2)}) copy-start(s32[2,128]{1,0:T(2,128)} %param.8) | copy-start | bytes 3076
  130.2 105.5 %all-to-all-start = ((bf16[16,1,128,1024]{3,2,1,0:T(8,128)(2,1)}), bf16[16,1,128,1024]{3,2,1,0:T(8,128)(2,1)}, u32[]{:S(2)}, u32[]{:S(2)}) async-start(bf16[16,1,128,1024]{3,2,1,0:T(8,128)(2,1)} %fusion), calls=%async_computation.1 | async-start | bytes 8388608 | tf_op jit(solution)/shard_map/all_to_all | solution.py:101
Sparse Core Ops, SparseCore 0:
  9.5 59.0 all-gather.3
  73.7 40.8 reduce-scatter.1
where the time goes:
time: 255 us; the launch traced here: 254 us
  waiting for transfers between devices  178 us (70%)
  local copies, waits for them, and re-layouts  21.3 us (8%)
  blocking collectives  13.8 us (5%)
  between operations  13.6 us (5%)
  starting transfers between devices  12 us (5%)
  other arithmetic  9.59 us (4%)
  matrix products  6.33 us (2%)
    all_to_all x1, waiting for transfers between devices, shards(): lax.all_to_all(parcel, 'dp', split_axis=0, concat_axis=0, tiled=True)  90.9 us
    all_gather x1, waiting for transfers between devices, project(): lax.all_gather(key_value_weight, 'fsdp', axis=1, tiled=True)  46.1 us
    reduce_scatter x1, waiting for transfers between devices, project(): lax.psum_scatter(partial_value, 'tensor', scatter_dimension=1, tiled=True)  40.1 us
    all_gather x1, blocking collectives, total_of_pieces(): parts = lax.all_gather(array, axis)  13.8 us
    all_to_all x1, starting transfers between devices, shards(): lax.all_to_all(parcel, 'dp', split_axis=0, concat_axis=0, tiled=True)  11.9 us
    unnamed x9, local copies, waits for them, and re-layouts  6.94 us
    gather x4, local copies, waits for them, and re-layouts, unpack_rows(): return jnp.take(flat, keep_index, axis=0)  5.95 us
    gather x3, local copies, waits for them, and re-layouts, pack_rows(): taken = jnp.take(flat_rows, send_index.reshape(-1), axis=0)  5.59 us
  transfers between devices with their start and end apart: 3, of which 3 were waited for; matrix products, arithmetic and copies ran while one was open for 2% of the time, Pallas kernels for 0%

commit v1 on v0

--- a/solution.py
+++ b/solution.py
@@ -5,6 +5,19 @@
 
 HEAD_SIZE = 128
 epsilon = 1e-05
+
+
+def cover_members_all(sheet, in_dim, z_in):
+    seen_now, latest = (sheet.shape[:in_dim], sheet.shape[in_dim + 1 :])
+    v_next = jnp.moveaxis(sheet.reshape(*seen_now, z_in, -1, *latest), in_dim, 0)
+    return v_next
+
+
+def sectors_press(sample, array_dim):
+    top = list(sample.shape[1:])
+    top[array_dim] *= sample.shape[0]
+    then = jnp.moveaxis(sample, 0, array_dim).reshape(top)
+    return then
 
 
 def total_of_pieces(array, axis):
@@ -98,7 +111,23 @@
     local_kv = project(tokens, gain, key_value_weight)
     results = attend(queries, local_kv, segment_ids)
     parcel = pack_rows(send_index, send_valid, results.reshape(batches, -1), length)
-    arrived = lax.all_to_all(parcel, "dp", split_axis=0, concat_axis=0, tiled=True)
+
+    def get_set(x_in, axis_id, here_x, chunk):
+        q_next, w1 = (lax.axis_size(axis_id), lax.axis_index(axis_id))
+        out_arr = cover_members_all(x_in, here_x, q_next)
+        views = [out_arr[w1]]
+        nth = 1
+        while nth < q_next:
+            carry = out_arr[w1 ^ nth]
+            views.append(
+                lax.ppermute(carry, axis_id, perm=[(j0, j0 ^ nth) for j0 in range(q_next)])
+            )
+            nth += 1
+        out_arr = jnp.stack(views)[w1 ^ jnp.arange(q_next)]
+        after = sectors_press(out_arr, chunk)
+        return after
+
+    arrived = get_set(parcel, "dp", 0, 0)
     return unpack_rows(keep_index, arrived).reshape(batches * length, -1)
 
 

time: 255 us -> 309 us (1.21)
  starting transfers between devices: 12 us -> 98.9 us
  waiting for transfers between devices: 178 us -> 129 us
  local copies, waits for them, and re-layouts: 21.3 us -> 38.4 us
    ppermute x0 -> x15, starting transfers between devices: none -> 98.8 us  [get_set(): lax.ppermute(carry, axis_id, perm=[(j0, j0 ^ nth) for j0 in range(q_next)])]
    all_to_all x1 -> x0, waiting for transfers between devices: 90.9 us -> none  [shards(): lax.all_to_all(parcel, 'dp', split_axis=0, concat_axis=0, tiled=True)]
    ppermute x0 -> x15, waiting for transfers between devices: none -> 44.9 us  [get_set(): lax.ppermute(carry, axis_id, perm=[(j0, j0 ^ nth) for j0 in range(q_next)])]
    all_to_all x1 -> x0, starting transfers between devices: 11.9 us -> none  [shards(): lax.all_to_all(parcel, 'dp', split_axis=0, concat_axis=0, tiled=True)]
    unnamed x9 -> x23, local copies, waits for them, and re-layouts: 6.94 us -> 17.1 us
    gather x0 -> x1, local copies, waits for them, and re-layouts: none -> 4.97 us  [get_set(): out_arr = jnp.stack(views)[w1 ^ jnp.arange(q_next)]]
  transfers between devices with their start and end apart: 3 -> 17, of which waited for: 3 -> 9; matrix products, arithmetic and copies ran while one was open for 2% -> 5% of each run, Pallas kernels for 0% -> 0%
where the time goes in v1:
time: 309 us; the launch traced here: 308 us
  waiting for transfers between devices  129 us (42%)
  starting transfers between devices  98.9 us (32%)
  local copies, waits for them, and re-layouts  38.4 us (12%)
  blocking collectives  13.8 us (4%)
  between operations  13.8 us (4%)
  other arithmetic  7.43 us (2%)
  matrix products  6.33 us (2%)
    ppermute x15, starting transfers between devices, get_set(): lax.ppermute(carry, axis_id, perm=[(j0, j0 ^ nth) for j0 in range(q_next)])  98.8 us
    all_gather x1, waiting for transfers between devices, project(): lax.all_gather(key_value_weight, 'fsdp', axis=1, tiled=True)  46.1 us
    ppermute x15, waiting for transfers between devices, get_set(): lax.ppermute(carry, axis_id, perm=[(j0, j0 ^ nth) for j0 in range(q_next)])  44.9 us
    reduce_scatter x1, waiting for transfers between devices, project(): lax.psum_scatter(partial_value, 'tensor', scatter_dimension=1, tiled=True)  37.5 us
    unnamed x23, local copies, waits for them, and re-layouts  17.1 us
    all_gather x1, blocking collectives, total_of_pieces(): parts = lax.all_gather(array, axis)  13.8 us
  transfers between devices with their start and end apart: 17, of which 9 were waited for; matrix products, arithmetic and copies ran while one was open for 5% of the time, Pallas kernels for 0%

profile of v1, /device:TPU:1, one launch (start us, length us, event | category | flops | bytes accessed | tf_op | source)
XLA Modules:
  0.0 308.0 jit_solution(8386668431371961148)
XLA Ops:
  8.5 13.8 %all-gather.1 = f32[8,1,256]{2,1,0:T(1,128)S(1)} all-gather(f32[1,1,256]{2,1,0:T(1,128)S(1)} %bitcast.122), channel_id=2, replica_groups=mesh['dp'=16,'fsdp'=4,'tensor'=8] {'tensor'}, dimensions={0}, use_global_device_ids=true | all-gather | bytes 9216 | tf_op jit(solution)/shard_map/all_gather | solution.py:24
  22.4 46.1 %all-gather.4.cloned.1.call-done = bf16[1024,2048]{1,0:T(8,128)(2,1)} async-done(((bf16[1024,512]{1,0:T(8,128)(2,1)}), bf16[1024,2048]{1,0:T(8,128)(2,1)}) %all-gather.4.cloned.1.call-update) | async-done | bytes 4194320 | tf_op jit(solution)/shard_map/all_gather | solution.py:49
  68.5 5.0 %fusion.7 = f32[256,2048]{1,0:T(8,128)} fusion(bf16[1024,2048]{1,0:T(8,128)(2,1)} %all-gather.4.cloned.1.call-done, bf16[256,1024]{1,0:T(8,128)(2,1)} %param.6, f32[1024]{0:T(1024)} %param.9, f32[256]{0:T(256)S(1)} %add_rsqrt_fusion), kind=kOutput, calls=%fused_computation.21 | convolution fusion | flops 1074790400 | bytes 6820864 | tf_op jit(solution)/shard_map/dot_general | solution.py:47
  77.2 37.5 %reduce-scatter.2.cloned.1.call-done = f32[256,256]{1,0:T(8,128)} async-done(((f32[256,2048]{1,0:T(8,128)}), f32[256,256]{1,0:T(8,128)}) %reduce-scatter.2.cloned.1.call-update) | async-done | bytes 262160 | tf_op jit(solution)/shard_map/reduce_scatter | solution.py:52
  118.3 1.9 gather_fusion.2
  120.2 3.3 %gather_fusion.3 = bf16[16,65536]{1,0:T(8,128)(2,1)} fusion(bf16[2,65536]{1,0:T(2,128)(2,1)S(1)} %get-tuple-element.30, s32[1024]{0:T(1024)S(1)} %get-tuple-element.36), kind=kCustom, calls=%fused_computation.3 | custom fusion | bytes 4194368 | tf_op jit(solution)/shard_map/jit(_take)/gather | solution.py:31
  123.5 1.9 pad_maximum_fusion
  125.4 2.3 copy.35
  129.4 6.4 %collective-permute-start = (bf16[1,1,128,1024]{3,2,1,0:T(8,128)(2,1)S(1)}, bf16[1,1,128,1024]{3,2,1,0:T(8,128)(2,1)S(1)}, u32[]{:S(2)}, u32[]{:S(2)}) collective-permute-start(bf16[1,1,128,1024]{3,2,1,0:T(8,128)(2,1)S(1)} %get-tuple-element.27), channel_id=1, source_target_pairs={{0,32},{32,0},{64,96},{96,64},{128,160},{160,128},{192,224},{224,1... | collective-permute-start | bytes 786440 | tf_op jit(solution)/shard_map/ppermute | solution.py:123
  135.8 3.6 %collective-permute-start.1 = (bf16[1,1,128,1024]{3,2,1,0:T(8,128)(2,1)S(1)}, bf16[1,1,128,1024]{3,2,1,0:T(8,128)(2,1)S(1)}, u32[]{:S(2)}, u32[]{:S(2)}) collective-permute-start(bf16[1,1,128,1024]{3,2,1,0:T(8,128)(2,1)S(1)} %get-tuple-element.26), channel_id=1, source_target_pairs={{0,64},{32,96},{64,0},{96,32},{128,192},{160,224},{192,128},{224,1... | collective-permute-start | bytes 786440 | tf_op jit(solution)/shard_map/ppermute | solution.py:123
  139.4 1.9 collective-permute-start.2
  141.4 4.6 %collective-permute-start.3 = (bf16[1,1,128,1024]{3,2,1,0:T(8,128)(2,1)S(1)}, bf16[1,1,128,1024]{3,2,1,0:T(8,128)(2,1)S(1)}, u32[]{:S(2)}, u32[]{:S(2)}) collective-permute-start(bf16[1,1,128,1024]{3,2,1,0:T(8,128)(2,1)S(1)} %get-tuple-element.24), channel_id=1, source_target_pairs={{0,128},{32,160},{64,192},{96,224},{128,0},{160,32},{192,64},{224,... | collective-permute-start | bytes 786440 | tf_op jit(solution)/shard_map/ppermute | solution.py:123
  146.0 2.1 collective-permute-start.4
  148.1 5.2 %collective-permute-start.5 = (bf16[1,1,128,1024]{3,2,1,0:T(8,128)(2,1)S(1)}, bf16[1,1,128,1024]{3,2,1,0:T(8,128)(2,1)S(1)}, u32[]{:S(2)}, u32[]{:S(2)}) collective-permute-start(bf16[1,1,128,1024]{3,2,1,0:T(8,128)(2,1)S(1)} %get-tuple-element.22), channel_id=1, source_target_pairs={{0,192},{32,224},{64,128},{96,160},{128,64},{160,96},{192,0},{224,... | collective-permute-start | bytes 786440 | tf_op jit(solution)/shard_map/ppermute | solution.py:123
  154.1 2.3 collective-permute-start.6
  158.9 5.6 %collective-permute-start.7 = (bf16[1,1,128,1024]{3,2,1,0:T(8,128)(2,1)S(1)}, bf16[1,1,128,1024]{3,2,1,0:T(8,128)(2,1)S(1)}, u32[]{:S(2)}, u32[]{:S(2)}) collective-permute-start(bf16[1,1,128,1024]{3,2,1,0:T(8,128)(2,1)S(1)} %get-tuple-element.20), channel_id=1, source_target_pairs={{0,256},{32,288},{64,320},{96,352},{128,384},{160,416},{192,448},{... | collective-permute-start | bytes 786440 | tf_op jit(solution)/shard_map/ppermute | solution.py:123
  165.2 32.5 %collective-permute-start.8 = (bf16[1,1,128,1024]{3,2,1,0:T(8,128)(2,1)S(1)}, bf16[1,1,128,1024]{3,2,1,0:T(8,128)(2,1)S(1)}, u32[]{:S(2)}, u32[]{:S(2)}) collective-permute-start(bf16[1,1,128,1024]{3,2,1,0:T(8,128)(2,1)S(1)} %get-tuple-element.19), channel_id=1, source_target_pairs={{0,288},{32,256},{64,352},{96,320},{128,416},{160,384},{192,480},{... | collective-permute-start | bytes 786440 | tf_op jit(solution)/shard_map/ppermute | solution.py:123
  198.5 3.0 collective-permute-done.4
  201.5 1.9 collective-permute-start.9
  204.1 18.0 %collective-permute-start.10 = (bf16[1,1,128,1024]{3,2,1,0:T(8,128)(2,1)S(1)}, bf16[1,1,128,1024]{3,2,1,0:T(8,128)(2,1)S(1)}, u32[]{:S(2)}, u32[]{:S(2)}) collective-permute-start(bf16[1,1,128,1024]{3,2,1,0:T(8,128)(2,1)S(1)} %get-tuple-element.17), channel_id=1, source_target_pairs={{0,352},{32,320},{64,288},{96,256},{128,480},{160,448},{192,416},{... | collective-permute-start | bytes 786440 | tf_op jit(solution)/shard_map/ppermute | solution.py:123
  222.9 3.0 collective-permute-start.11
  226.6 3.4 %collective-permute-start.12 = (bf16[1,1,128,1024]{3,2,1,0:T(8,128)(2,1)S(1)}, bf16[1,1,128,1024]{3,2,1,0:T(8,128)(2,1)S(1)}, u32[]{:S(2)}, u32[]{:S(2)}) collective-permute-start(bf16[1,1,128,1024]{3,2,1,0:T(8,128)(2,1)S(1)} %get-tuple-element.15), channel_id=1, source_target_pairs={{0,416},{32,384},{64,480},{96,448},{128,288},{160,256},{192,352},{... | collective-permute-start | bytes 786440 | tf_op jit(solution)/shard_map/ppermute | solution.py:123
  230.8 2.1 collective-permute-start.13
  233.6 6.1 %collective-permute-start.14 = (bf16[1,1,128,1024]{3,2,1,0:T(8,128)(2,1)S(1)}, bf16[1,1,128,1024]{3,2,1,0:T(8,128)(2,1)S(1)}, u32[]{:S(2)}, u32[]{:S(2)}) collective-permute-start(bf16[1,1,128,1024]{3,2,1,0:T(8,128)(2,1)S(1)} %get-tuple-element.13), channel_id=1, source_target_pairs={{0,480},{32,448},{64,416},{96,384},{128,352},{160,320},{192,288},{... | collective-permute-start | bytes 786440 | tf_op jit(solution)/shard_map/ppermute | solution.py:123
  240.4 19.5 %collective-permute-done.10 = bf16[1,1,128,1024]{3,2,1,0:T(8,128)(2,1)S(1)} collective-permute-done((bf16[1,1,128,1024]{3,2,1,0:T(8,128)(2,1)S(1)}, bf16[1,1,128,1024]{3,2,1,0:T(8,128)(2,1)S(1)}, u32[]{:S(2)}, u32[]{:S(2)}) %collective-permute-start.10) | collective-permute-done | bytes 262176 | tf_op jit(solution)/shard_map/ppermute | solution.py:123
  260.6 4.9 %collective-permute-done.11 = bf16[1,1,128,1024]{3,2,1,0:T(8,128)(2,1)S(1)} collective-permute-done((bf16[1,1,128,1024]{3,2,1,0:T(8,128)(2,1)S(1)}, bf16[1,1,128,1024]{3,2,1,0:T(8,128)(2,1)S(1)}, u32[]{:S(2)}, u32[]{:S(2)}) %collective-permute-start.11) | collective-permute-done | bytes 262176 | tf_op jit(solution)/shard_map/ppermute | solution.py:123
  266.2 4.9 %collective-permute-done.12 = bf16[1,1,128,1024]{3,2,1,0:T(8,128)(2,1)S(1)} collective-permute-done((bf16[1,1,128,1024]{3,2,1,0:T(8,128)(2,1)S(1)}, bf16[1,1,128,1024]{3,2,1,0:T(8,128)(2,1)S(1)}, u32[]{:S(2)}, u32[]{:S(2)}) %collective-permute-start.12) | collective-permute-done | bytes 262176 | tf_op jit(solution)/shard_map/ppermute | solution.py:123
  271.8 7.1 %collective-permute-done.13 = bf16[1,1,128,1024]{3,2,1,0:T(8,128)(2,1)S(1)} collective-permute-done((bf16[1,1,128,1024]{3,2,1,0:T(8,128)(2,1)S(1)}, bf16[1,1,128,1024]{3,2,1,0:T(8,128)(2,1)S(1)}, u32[]{:S(2)}, u32[]{:S(2)}) %collective-permute-start.13) | collective-permute-done | bytes 262176 | tf_op jit(solution)/shard_map/ppermute | solution.py:123
  279.6 4.0 %collective-permute-done.14 = bf16[1,1,128,1024]{3,2,1,0:T(8,128)(2,1)S(1)} collective-permute-done((bf16[1,1,128,1024]{3,2,1,0:T(8,128)(2,1)S(1)}, bf16[1,1,128,1024]{3,2,1,0:T(8,128)(2,1)S(1)}, u32[]{:S(2)}, u32[]{:S(2)}) %collective-permute-start.14) | collective-permute-done | bytes 262176 | tf_op jit(solution)/shard_map/ppermute | solution.py:123
  284.3 5.0 %gather_fusion.1 = bf16[16,128,1024]{2,1,0:T(8,128)(2,1)} fusion(bf16[16,128,1024]{2,1,0:T(8,128)(2,1)} %bitcast.46, s32[1024]{0:T(1024)S(1)} %pad_clamp_fusion.1), kind=kCustom, calls=%fused_computation.1 | custom fusion | bytes 8388672 | tf_op jit(solution)/shard_map/gather | solution.py:126
  289.3 4.5 %copy.36 = bf16[2,8,128,1024]{3,1,2,0:T(8,128)(2,1)S(1)} copy(bf16[2,8,128,1024]{3,2,1,0:T(8,128)(2,1)} %bitcast.117) | data formatting | bytes 8388608
  295.4 3.0 gather_fusion.4
  (78 shorter events, 27.7 us)
Async XLA Ops:
  6.5 62.0 %all-gather.4.cloned.1.call-start = ((), (), s32[]{:S(2)}) async-start(), calls=%async_computation.1 | async-start | bytes 5242880 | tf_op jit(solution)/shard_map/all_gather | solution.py:49
  7.3 107.4 %reduce-scatter.2.cloned.1.call-start = ((), (), s32[]{:S(2)}) async-start(), calls=%async_computation.2 | async-start | bytes 2359296 | tf_op jit(solution)/shard_map/reduce_scatter | solution.py:52
  22.4 51.3 %copy-start.2 = (s32[32]{0:T(128)S(1)}, s32[32]{0:T(128)}, u32[]{:S(2)}) copy-start(s32[32]{0:T(128)} %param.11) | copy-start | bytes 388
  22.4 53.3 %copy-start = (bf16[256,1024]{1,0:T(8,128)(2,1)S(1)}, bf16[256,1024]{1,0:T(8,128)(2,1)}, u32[]{:S(2)}) copy-start(bf16[256,1024]{1,0:T(8,128)(2,1)} %param.7) | copy-start | bytes 1572868
  22.4 54.6 %copy-start.1 = (s32[2,128]{1,0:T(2,128)S(1)}, s32[2,128]{1,0:T(2,128)}, u32[]{:S(2)}) copy-start(s32[2,128]{1,0:T(2,128)} %param.8) | copy-start | bytes 3076
  129.4 18.8 %collective-permute-start = (bf16[1,1,128,1024]{3,2,1,0:T(8,128)(2,1)S(1)}, bf16[1,1,128,1024]{3,2,1,0:T(8,128)(2,1)S(1)}, u32[]{:S(2)}, u32[]{:S(2)}) collective-permute-start(bf16[1,1,128,1024]{3,2,1,0:T(8,128)(2,1)S(1)} %get-tuple-element.27), channel_id=1, source_target_pairs={{0,32},{32,0},{64,96},{96,64},{128,160},{160,128},{192,224},{224,1... | collective-permute-start | bytes 786440 | tf_op jit(solution)/shard_map/ppermute | solution.py:123
  135.8 18.3 %collective-permute-start.1 = (bf16[1,1,128,1024]{3,2,1,0:T(8,128)(2,1)S(1)}, bf16[1,1,128,1024]{3,2,1,0:T(8,128)(2,1)S(1)}, u32[]{:S(2)}, u32[]{:S(2)}) collective-permute-start(bf16[1,1,128,1024]{3,2,1,0:T(8,128)(2,1)S(1)} %get-tuple-element.26), channel_id=1, source_target_pairs={{0,64},{32,96},{64,0},{96,32},{128,192},{160,224},{192,128},{224,1... | collective-permute-start | bytes 786440 | tf_op jit(solution)/shard_map/ppermute | solution.py:123
  139.4 19.4 %collective-permute-start.2 = (bf16[1,1,128,1024]{3,2,1,0:T(8,128)(2,1)S(1)}, bf16[1,1,128,1024]{3,2,1,0:T(8,128)(2,1)S(1)}, u32[]{:S(2)}, u32[]{:S(2)}) collective-permute-start(bf16[1,1,128,1024]{3,2,1,0:T(8,128)(2,1)S(1)} %get-tuple-element.25), channel_id=1, source_target_pairs={{0,96},{32,64},{64,32},{96,0},{128,224},{160,192},{192,160},{224,1... | collective-permute-start | bytes 786440 | tf_op jit(solution)/shard_map/ppermute | solution.py:123
  141.4 23.9 %collective-permute-start.3 = (bf16[1,1,128,1024]{3,2,1,0:T(8,128)(2,1)S(1)}, bf16[1,1,128,1024]{3,2,1,0:T(8,128)(2,1)S(1)}, u32[]{:S(2)}, u32[]{:S(2)}) collective-permute-start(bf16[1,1,128,1024]{3,2,1,0:T(8,128)(2,1)S(1)} %get-tuple-element.24), channel_id=1, source_target_pairs={{0,128},{32,160},{64,192},{96,224},{128,0},{160,32},{192,64},{224,... | collective-permute-start | bytes 786440 | tf_op jit(solution)/shard_map/ppermute | solution.py:123
  146.0 55.5 %collective-permute-start.4 = (bf16[1,1,128,1024]{3,2,1,0:T(8,128)(2,1)S(1)}, bf16[1,1,128,1024]{3,2,1,0:T(8,128)(2,1)S(1)}, u32[]{:S(2)}, u32[]{:S(2)}) collective-permute-start(bf16[1,1,128,1024]{3,2,1,0:T(8,128)(2,1)S(1)} %get-tuple-element.23), channel_id=1, source_target_pairs={{0,160},{32,128},{64,224},{96,192},{128,32},{160,0},{192,96},{224,... | collective-permute-start | bytes 786440 | tf_op jit(solution)/shard_map/ppermute | solution.py:123
  148.1 56.0 %collective-permute-start.5 = (bf16[1,1,128,1024]{3,2,1,0:T(8,128)(2,1)S(1)}, bf16[1,1,128,1024]{3,2,1,0:T(8,128)(2,1)S(1)}, u32[]{:S(2)}, u32[]{:S(2)}) collective-permute-start(bf16[1,1,128,1024]{3,2,1,0:T(8,128)(2,1)S(1)} %get-tuple-element.22), channel_id=1, source_target_pairs={{0,192},{32,224},{64,128},{96,160},{128,64},{160,96},{192,0},{224,... | collective-permute-start | bytes 786440 | tf_op jit(solution)/shard_map/ppermute | solution.py:123
  154.1 68.8 %collective-permute-start.6 = (bf16[1,1,128,1024]{3,2,1,0:T(8,128)(2,1)S(1)}, bf16[1,1,128,1024]{3,2,1,0:T(8,128)(2,1)S(1)}, u32[]{:S(2)}, u32[]{:S(2)}) collective-permute-start(bf16[1,1,128,1024]{3,2,1,0:T(8,128)(2,1)S(1)} %get-tuple-element.21), channel_id=1, source_target_pairs={{0,224},{32,192},{64,160},{96,128},{128,96},{160,64},{192,32},{224... | collective-permute-start | bytes 786440 | tf_op jit(solution)/shard_map/ppermute | solution.py:123
  158.9 67.7 %collective-permute-start.7 = (bf16[1,1,128,1024]{3,2,1,0:T(8,128)(2,1)S(1)}, bf16[1,1,128,1024]{3,2,1,0:T(8,128)(2,1)S(1)}, u32[]{:S(2)}, u32[]{:S(2)}) collective-permute-start(bf16[1,1,128,1024]{3,2,1,0:T(8,128)(2,1)S(1)} %get-tuple-element.20), channel_id=1, source_target_pairs={{0,256},{32,288},{64,320},{96,352},{128,384},{160,416},{192,448},{... | collective-permute-start | bytes 786440 | tf_op jit(solution)/shard_map/ppermute | solution.py:123
  165.2 65.5 %collective-permute-start.8 = (bf16[1,1,128,1024]{3,2,1,0:T(8,128)(2,1)S(1)}, bf16[1,1,128,1024]{3,2,1,0:T(8,128)(2,1)S(1)}, u32[]{:S(2)}, u32[]{:S(2)}) collective-permute-start(bf16[1,1,128,1024]{3,2,1,0:T(8,128)(2,1)S(1)} %get-tuple-element.19), channel_id=1, source_target_pairs={{0,288},{32,256},{64,352},{96,320},{128,416},{160,384},{192,480},{... | collective-permute-start | bytes 786440 | tf_op jit(solution)/shard_map/ppermute | solution.py:123
  201.5 32.1 %collective-permute-start.9 = (bf16[1,1,128,1024]{3,2,1,0:T(8,128)(2,1)S(1)}, bf16[1,1,128,1024]{3,2,1,0:T(8,128)(2,1)S(1)}, u32[]{:S(2)}, u32[]{:S(2)}) collective-permute-start(bf16[1,1,128,1024]{3,2,1,0:T(8,128)(2,1)S(1)} %get-tuple-element.18), channel_id=1, source_target_pairs={{0,320},{32,352},{64,256},{96,288},{128,448},{160,480},{192,384},{... | collective-permute-start | bytes 786440 | tf_op jit(solution)/shard_map/ppermute | solution.py:123
  204.1 55.8 %collective-permute-start.10 = (bf16[1,1,128,1024]{3,2,1,0:T(8,128)(2,1)S(1)}, bf16[1,1,128,1024]{3,2,1,0:T(8,128)(2,1)S(1)}, u32[]{:S(2)}, u32[]{:S(2)}) collective-permute-start(bf16[1,1,128,1024]{3,2,1,0:T(8,128)(2,1)S(1)} %get-tuple-element.17), channel_id=1, source_target_pairs={{0,352},{32,320},{64,288},{96,256},{128,480},{160,448},{192,416},{... | collective-permute-start | bytes 786440 | tf_op jit(solution)/shard_map/ppermute | solution.py:123
  222.9 42.6 %collective-permute-start.11 = (bf16[1,1,128,1024]{3,2,1,0:T(8,128)(2,1)S(1)}, bf16[1,1,128,1024]{3,2,1,0:T(8,128)(2,1)S(1)}, u32[]{:S(2)}, u32[]{:S(2)}) collective-permute-start(bf16[1,1,128,1024]{3,2,1,0:T(8,128)(2,1)S(1)} %get-tuple-element.16), channel_id=1, source_target_pairs={{0,384},{32,416},{64,448},{96,480},{128,256},{160,288},{192,320},{... | collective-permute-start | bytes 786440 | tf_op jit(solution)/shard_map/ppermute | solution.py:123
  226.6 44.5 %collective-permute-start.12 = (bf16[1,1,128,1024]{3,2,1,0:T(8,128)(2,1)S(1)}, bf16[1,1,128,1024]{3,2,1,0:T(8,128)(2,1)S(1)}, u32[]{:S(2)}, u32[]{:S(2)}) collective-permute-start(bf16[1,1,128,1024]{3,2,1,0:T(8,128)(2,1)S(1)} %get-tuple-element.15), channel_id=1, source_target_pairs={{0,416},{32,384},{64,480},{96,448},{128,288},{160,256},{192,352},{... | collective-permute-start | bytes 786440 | tf_op jit(solution)/shard_map/ppermute | solution.py:123
  230.8 48.1 %collective-permute-start.13 = (bf16[1,1,128,1024]{3,2,1,0:T(8,128)(2,1)S(1)}, bf16[1,1,128,1024]{3,2,1,0:T(8,128)(2,1)S(1)}, u32[]{:S(2)}, u32[]{:S(2)}) collective-permute-start(bf16[1,1,128,1024]{3,2,1,0:T(8,128)(2,1)S(1)} %get-tuple-element.14), channel_id=1, source_target_pairs={{0,448},{32,480},{64,384},{96,416},{128,320},{160,352},{192,256},{... | collective-permute-start | bytes 786440 | tf_op jit(solution)/shard_map/ppermute | solution.py:123
  233.6 50.0 %collective-permute-start.14 = (bf16[1,1,128,1024]{3,2,1,0:T(8,128)(2,1)S(1)}, bf16[1,1,128,1024]{3,2,1,0:T(8,128)(2,1)S(1)}, u32[]{:S(2)}, u32[]{:S(2)}) collective-permute-start(bf16[1,1,128,1024]{3,2,1,0:T(8,128)(2,1)S(1)} %get-tuple-element.13), channel_id=1, source_target_pairs={{0,480},{32,448},{64,416},{96,384},{128,352},{160,320},{192,288},{... | collective-permute-start | bytes 786440 | tf_op jit(solution)/shard_map/ppermute | solution.py:123
Sparse Core Ops, SparseCore 0:
  9.5 59.0 all-gather.3
  73.7 40.9 reduce-scatter.1
